TPU v7x, 128 devices: a whole 4x4x4 slice. The times are simulated.
128 devices in a mesh: seq: 16 (over y, x_lo, core), tensor: 8 (over z, x_hi).
Axes of the slice: x: 4 (x_hi: 2, x_lo: 2; x = x_hi * 2 + x_lo), y: 4, z: 4, core: 2. Of those that a mesh axis runs over, the one named last changes fastest.
Arguments:
- tokens: bfloat16 [2048, 16384], P('seq', 'tensor'), may hold values from -100 to 100
- norm_gain: float32 [16384], P('tensor'), may hold values from 0.5 to 1.5
- projection_weight: bfloat16 [2048, 16384], P('tensor', 'seq'), may hold values from -1.5 to 1.5
- panel_index: int32 [1], replicated, may hold values from 0 to 31
Outputs:
- gram: float32 [16384, 16384], P('seq', 'tensor')
- factor_panel: bfloat16 [16384, 512], P('seq')
- projected: float32 [2048, 512], P('tensor', 'seq')
All inputs are finite; a program needn't handle non-finite values.
Results may differ from a plain program's by a relative error of at most 0.0057.
Values may be sent and summed in bfloat16 or wider, within the bound.
A program may use at most 128 MiB of HBM per device.

v0:
```python
import jax
import jax.numpy as jnp
from jax import lax
from jax.sharding import PartitionSpec as P

D = 16384
PANEL = 512


epsilon = 1e-05
damping = 0.1


def broadcast(value, axis, source):
    kept = jnp.where(lax.axis_index(axis) == source, value, 0).astype(value.dtype)
    return lax.psum(kept, axis)


def on_device(tokens, norm_gain, projection_weight, panel_index):
    token_values = tokens.astype(jnp.float32)
    squares = lax.psum(jnp.sum(token_values * token_values, axis=1), "tensor")
    scaled = token_values * lax.rsqrt(squares / D + epsilon)[:, None] * norm_gain[None, :]
    normed = scaled.astype(jnp.bfloat16)
    column_width = normed.shape[1]
    row_width = column_width * lax.axis_size("tensor") // lax.axis_size("seq")
    blocks = column_width // row_width
    seq_index = lax.axis_index("seq")
    tensor_index = lax.axis_index("tensor")
    columns = lax.all_gather(normed, "seq", axis=0, tiled=True)
    local_rows = lax.dynamic_slice_in_dim(columns, seq_index % blocks * row_width, row_width, 1)
    row_part = broadcast(local_rows, "tensor", seq_index // blocks)
    tokens_all = columns.shape[0]
    gram_tile = (
        lax.dot_general(
            row_part, columns, (((0,), (0,)), ((), ())), preferred_element_type=jnp.float32
        )
        / tokens_all
    )
    normed_wide = normed.astype(jnp.float32)
    trace_sum = lax.psum(jnp.sum(normed_wide * normed_wide), ("seq", "tensor")) / tokens_all
    diag_shift = damping * trace_sum / D
    row_ids = seq_index * row_width + lax.iota(jnp.int32, row_width)
    col_ids = tensor_index * column_width + lax.iota(jnp.int32, column_width)
    shifted = gram_tile + jnp.where(
        row_ids[:, None] == col_ids[None, :], diag_shift, jnp.float32(0.0)
    )
    panel_start = panel_index[0] * PANEL
    owner_column = panel_start // column_width
    offset = panel_start - owner_column * column_width
    panel_rows = lax.dynamic_slice_in_dim(shifted, offset, PANEL, 1)
    piece_rows = min(PANEL, row_width)
    global_row = panel_start + 0
    source = global_row // row_width
    local_offset = global_row - source * row_width
    piece = lax.dynamic_slice_in_dim(panel_rows, local_offset, piece_rows, 0)
    pieces = broadcast(piece, "seq", source)
    diag_block = pieces
    identity = jnp.eye(PANEL, dtype=jnp.float32)
    diag_block = jnp.where(tensor_index == owner_column, diag_block, identity)
    factor = jnp.linalg.cholesky(diag_block)
    solved = lax.linalg.triangular_solve(
        factor, panel_rows, left_side=False, lower=True, transpose_a=True
    )
    whitened_rows = solved.astype(jnp.bfloat16)
    whitened_full = broadcast(whitened_rows, "tensor", owner_column)
    partial_value = jnp.dot(projection_weight, whitened_full, preferred_element_type=jnp.float32)
    projected = lax.psum_scatter(partial_value, "seq", scatter_dimension=1, tiled=True)
    return (shifted, whitened_full, projected)


def solution(mesh):
    placed = (P("seq", "tensor"), P("tensor"), P("tensor", "seq"), P())
    return jax.shard_map(
        on_device,
        mesh=mesh,
        in_specs=placed,
        out_specs=(P("seq", "tensor"), P("seq", None), P("tensor", "seq")),
        check_vma=False,
    )
```

profile of v0, /device:TPU:1, one launch (start us, length us, event | category | flops | bytes accessed | tf_op | source)
XLA Modules:
  0.0 739.4 jit_solution(978973545675533625)
XLA Ops:
  8.5 22.6 %psum.35 = f32[128]{0:T(128)S(1)} all-reduce(f32[128]{0:T(128)S(1)} %fusion.9), channel_id=1, replica_groups=mesh['seq'=16,'tensor'=8] {'tensor'}, use_global_device_ids=true, to_apply=%region_1.0 | all-reduce | flops 128 | bytes 1024 | tf_op jit(solution)/shard_map/psum | solution.py:21
  31.1 2.7 multiply_reduce_fusion
  33.9 52.8 %all-gather.2.cloned.1.call-done = bf16[2048,2048]{1,0:T(8,128)(2,1)} async-done(((bf16[128,2048]{1,0:T(8,128)(2,1)}), bf16[2048,2048]{1,0:T(8,128)(2,1)}) %all-gather.2.cloned.1.call-update) | async-done | bytes 8388624 | tf_op jit(solution)/shard_map/all_gather | solution.py:29
  86.7 5.4 dynamic-slice_select_fusion
  92.2 209.0 %psum.37 = f32[]{:T(128)} all-reduce(f32[]{:T(128)} %get-tuple-element.26), channel_id=1, replica_groups=mesh['seq'=16,'tensor'=8] {'seq','tensor'}, use_global_device_ids=true, to_apply=%region_4.5 | all-reduce | flops 1 | bytes 8 | tf_op jit(solution)/shard_map/psum | solution.py:40
  302.6 13.0 %select_add_fusion = f32[1024,2048]{0,1:T(8,128)S(1)} fusion(bf16[2048,1024]{1,0:T(8,128)(2,1)} %all-reduce.5.cloned.1.call-done, bf16[2048,2048]{1,0:T(8,128)(2,1)} %all-gather.2.cloned.1.call-done, f32[]{:T(128)S(6)} %div.53, s32[1024]{0:T(1024)S(1)} %iota_add_fusion.1, s32[2048]{0:T(1024)S(1)} %iota_add_fusion), kind=kOutput, calls=%fused_computation.2 | convolution fusion | flops 8598323200 | bytes 20983812 | tf_op jit(solution)/shard_map/dot_general | solution.py:34
  315.7 3.2 copy-done.1
  320.8 116.3 %all-reduce.7.cloned.1.call-done = f32[512,512]{0,1:T(8,128)} async-done(((f32[512,512]{0,1:T(8,128)}), f32[512,512]{0,1:T(8,128)}) %all-reduce.7.cloned.1.call-update) | async-done | bytes 1048592 | tf_op jit(solution)/shard_map/psum | solution.py:16
  440.0 11.7 %cholesky.103 = f32[128,128]{1,0:T(8,128)S(1)} custom-call(f32[128,128]{1,0:T(8,128)S(1)} %cholesky.263), custom_call_target="Cholesky" | custom-call | tf_op jit(solution)/shard_map/jit(cholesky)/cholesky | solution.py:60
  451.8 9.8 %custom-call.30 = f32[1,128,128]{1,2,0:T(8,128)S(1)} custom-call(f32[1,128,128]{2,1,0:T(8,128)S(1)} %get-tuple-element.35), custom_call_target="InvertDiagBlocksLowerTriangular" | custom-call | tf_op jit(solution)/shard_map/jit(cholesky)/cholesky | solution.py:60
  462.3 11.7 %cholesky.215 = f32[128,128]{1,0:T(8,128)S(1)} custom-call(f32[128,128]{1,0:T(8,128)S(1)} %cholesky.267), custom_call_target="Cholesky" | custom-call | tf_op jit(solution)/shard_map/jit(cholesky)/cholesky | solution.py:60
  474.4 9.9 %custom-call.31 = f32[1,128,128]{1,2,0:T(8,128)S(1)} custom-call(f32[1,128,128]{2,1,0:T(8,128)S(1)} %get-tuple-element.33), custom_call_target="InvertDiagBlocksLowerTriangular" | custom-call | tf_op jit(solution)/shard_map/jit(cholesky)/cholesky | solution.py:60
  485.4 11.7 %cholesky.236 = f32[128,128]{1,0:T(8,128)S(1)} custom-call(f32[128,128]{1,0:T(8,128)S(1)} %cholesky.272), custom_call_target="Cholesky" | custom-call | tf_op jit(solution)/shard_map/jit(cholesky)/cholesky | solution.py:60
  497.3 9.8 %custom-call.32 = f32[1,128,128]{1,2,0:T(8,128)S(1)} custom-call(f32[1,128,128]{2,1,0:T(8,128)S(1)} %get-tuple-element.31), custom_call_target="InvertDiagBlocksLowerTriangular" | custom-call | tf_op jit(solution)/shard_map/jit(cholesky)/cholesky | solution.py:60
  507.9 11.9 %cholesky.253 = f32[128,128]{1,0:T(8,128)S(1)} custom-call(f32[128,128]{1,0:T(8,128)S(1)} %convolution_subtract_fusion.4), custom_call_target="Cholesky" | custom-call | tf_op jit(solution)/shard_map/jit(cholesky)/cholesky | solution.py:60
  524.5 8.5 %while.1 = (s32[]{:T(128)}, f32[512,512]{0,1:T(8,128)S(1)}, s32[4,2]{0,1:T(2,128)S(1)}, f32[4,128,128]{2,1,0:T(8,128)S(1)}, s32[]{:T(128)}) while((s32[]{:T(128)}, f32[512,512]{0,1:T(8,128)S(1)}, s32[4,2]{0,1:T(2,128)S(1)}, f32[4,128,128]{2,1,0:T(8,128)S(1)}, s32[]{:T(128)}) %tuple.33), condition=%wide.while_cond, body=%wide.while_body.sunk | while | flops 2 | bytes 393321 | solution.py:61
  532.9 39.3 %custom-call.33 = f32[4,128,128]{1,2,0:T(8,128)S(1)} custom-call(f32[4,128,128]{2,1,0:T(8,128)S(1)} %get-tuple-element.10), custom_call_target="InvertDiagBlocksLowerTriangular" | custom-call | tf_op jit(solution)/shard_map/triangular_solve | solution.py:61
  573.9 1.7 convolution_subtract_fusion.1
  576.2 1.8 convolution_subtract_fusion
  578.6 2.2 fusion.6
  582.7 86.8 %all-reduce.9.cloned.1.call-done = bf16[1024,512]{0,1:T(8,128)(2,1)} async-done(((bf16[1024,512]{0,1:T(8,128)(2,1)}), bf16[1024,512]{0,1:T(8,128)(2,1)}) %all-reduce.9.cloned.1.call-update) | async-done | bytes 1048592 | tf_op jit(solution)/shard_map/psum | solution.py:16
  669.6 2.5 convolution_bitcast_fusion
  672.1 9.2 %copy.17 = f32[1024,2048]{1,0:T(8,128)} copy(f32[1024,2048]{0,1:T(8,128)} %copy-done.1) | data formatting | bytes 16777216
  682.6 50.0 %reduce-scatter.2.cloned.1.call-done = f32[256,32]{0,1:T(8,128)} async-done(((f32[256,512]{0,1:T(8,128)}), f32[256,32]{0,1:T(8,128)}) %reduce-scatter.2.cloned.1.call-update) | async-done | bytes 32784 | tf_op jit(solution)/shard_map/reduce_scatter | solution.py:67
  (82 shorter events, 25.8 us)
Async XLA Ops:
  7.2 662.4 %copy-start = (bf16[256,1024]{1,0:T(8,128)(2,1)S(1)}, bf16[256,1024]{1,0:T(8,128)(2,1)}, u32[]{:S(2)}) copy-start(bf16[256,1024]{1,0:T(8,128)(2,1)} %param.6) | copy-start | bytes 1572868
  7.2 79.5 %all-gather.2.cloned.1.call-start = ((), (), s32[]{:S(2)}) async-start(), calls=%async_computation.1 | async-start | bytes 8912896 | tf_op jit(solution)/shard_map/all_gather | solution.py:29
  33.8 268.8 %all-reduce.5.cloned.1.call-start = ((), (), s32[]{:S(2)}) async-start(), calls=%async_computation.2 | async-start | bytes 8388608 | tf_op jit(solution)/shard_map/psum | solution.py:16
  92.1 345.0 %all-reduce.7.cloned.1.call-start = ((), (), s32[]{:S(2)}) async-start(), calls=%async_computation.3 | async-start | bytes 2097152 | tf_op jit(solution)/shard_map/psum | solution.py:16
  315.7 3.2 copy-start.1
  320.3 349.3 %all-reduce.9.cloned.1.call-start = ((), (), s32[]{:S(2)}) async-start(), calls=%async_computation.4 | async-start | bytes 2097152 | tf_op jit(solution)/shard_map/psum | solution.py:16
  437.1 1.4 copy-start.2
  582.7 149.9 %reduce-scatter.2.cloned.1.call-start = ((), (), s32[]{:S(2)}) async-start(), calls=%async_computation.5 | async-start | bytes 557056 | tf_op jit(solution)/shard_map/reduce_scatter | solution.py:67
  672.1 9.2 %copy-start.3 = (bf16[1024,512]{0,1:T(8,128)(2,1)S(1)}, bf16[1024,512]{0,1:T(8,128)(2,1)}, u32[]{:S(2)}) copy-start(bf16[1024,512]{0,1:T(8,128)(2,1)} %all-reduce.9.cloned.1.call-done) | copy-start | bytes 3145732
Sparse Core Ops, SparseCore 0:
  33.9 52.7 all-gather.1
  92.3 186.1 all-reduce.4
  320.4 116.6 all-reduce.6
  582.8 86.6 all-reduce.8
  672.5 60.1 reduce-scatter.1
where the time goes:
time: 749 us; the launch traced here: 739 us
  waiting for transfers between devices  306 us (41%)
  blocking collectives  232 us (31%)
  other arithmetic  132 us (18%)
  matrix products  27 us (4%)
  local copies, waits for them, and re-layouts  24.1 us (3%)
  between operations  18.2 us (2%)
    psum x1, blocking collectives, on_device(): lax.psum(jnp.sum(normed_wide * normed_wide), ('seq', 'tensor')) / tokens_all  209 us
    psum x3, waiting for transfers between devices, broadcast(): return lax.psum(kept, axis)  203 us
    another operation x14, other arithmetic, on_device(): factor = jnp.linalg.cholesky(diag_block)  78.6 us
    all_gather x1, waiting for transfers between devices, on_device(): columns = lax.all_gather(normed, 'seq', axis=0, tiled=True)  52.8 us
    reduce_scatter x1, waiting for transfers between devices, on_device(): lax.psum_scatter(partial_value, 'seq', scatter_dimension=1, tiled=True)  50 us
    another operation x3, other arithmetic, on_device(): lax.linalg.triangular_solve(factor, panel_rows, left_side=False, lower=Tr...  39.4 us
    psum x1, blocking collectives, on_device(): squares = lax.psum(jnp.sum(token_values * token_values, axis=1), 'tensor')  22.6 us
  transfers between devices with their start and end apart: 5, of which 4 were waited for; matrix products, arithmetic and copies ran while one was open for 1% of the time, Pallas kernels for 0%

commit v1 on v0

v1 whole, which is shorter than its diff:
```python
import functools

import jax
import jax.numpy as jnp
from jax import lax
from jax.experimental import pallas as pl
from jax.experimental.pallas import tpu as pltpu
from jax.sharding import PartitionSpec as P

D = 16384
PANEL = 512
TOKENS = 2048
EPSILON = 1e-05
DAMPING = 0.1
F32 = jnp.float32
BF16 = jnp.bfloat16
MESH = pl.DeviceIdType.MESH


def halves(a):
    high = a.astype(BF16)
    return high, (a - high.astype(F32)).astype(BF16)


def dot(a, b, dims):
    return lax.dot_general(a, b, (dims, ((), ())), preferred_element_type=F32)


def dot_split(a, b, dims):
    ah, al = halves(a)
    bh, bl = halves(b)
    return dot(ah, bh, dims) + (dot(ah, bl, dims) + dot(al, bh, dims))


def row_of(tile, r):
    return jnp.broadcast_to(tile[r : r + 1, :], (8, 128))


def column_of(tile, k):
    return jnp.broadcast_to(tile[:, k : k + 1], (8, 128))


def inverse_factor(a):
    sub = lax.broadcasted_iota(jnp.int32, (8, 128), 0)
    lane = lax.broadcasted_iota(jnp.int32, (8, 128), 1)
    inv = [jnp.where(sub + 8 * g == lane, 1.0, 0.0).astype(F32) for g in range(16)]
    for g in range(16):
        cols = [{k: column_of(a[k], 8 * g + c) for k in range(g, 16)} for c in range(8)]
        for c in range(8):
            r = lax.rsqrt(row_of(cols[c][g], c))
            m = {k: cols[c][k] * r for k in range(g, 16)}
            for c2 in range(c + 1, 8):
                f = row_of(cols[c2][g], c) * r
                for k in range(g, 16):
                    cols[c2][k] = cols[c2][k] - m[k] * f
            u = row_of(a[g], c) * r
            z = row_of(inv[g], c) * r
            m[g] = jnp.where(sub > c, m[g], 0.0)
            for k in range(g, 16):
                a[k] = a[k] - m[k] * u
                inv[k] = inv[k] - m[k] * z
            inv[g] = jnp.where(sub == c, z, inv[g])
    return inv


def kernel(
    tok, gain, index, weight,
    gram_out, panel_out, proj_out,
    cols, rows, panel, gram, ext, inverse, white, part, landed,
    flipped, squares, masked, sums, trace_own, trace_t, trace_s, trace_sum,
    sq_send, sq_recv, rs_send, rs_recv, ag_send, ag_recv, tt_send, tt_recv, ts_send, ts_recv,
    p_send, p_recv, c_send, c_recv, r_send, r_recv, x_send, x_recv, x_local,
    f_send, f_recv, out_sem, wh_sem,
):
    s, t = lax.axis_index("seq"), lax.axis_index("tensor")
    i, core = s // 2, s % 2
    y, xl = i // 2, i % 2
    z, xh = t // 2, t % 2
    own = i == t
    start = index[0] * PANEL

    def seq_peer(k):
        return (k, t)

    def tensor_peer(k):
        return (s, k)

    value = tok[...].astype(F32)
    part_sq = jnp.zeros((128, 128), F32)
    for b in range(16):
        piece = value[:, b * 128 : (b + 1) * 128]
        part_sq = part_sq + piece * piece
    tile = lax.dot_general(
        jnp.ones((8, 128), F32), part_sq, (((1,), (1,)), ((), ())),
        precision=lax.Precision.HIGHEST, preferred_element_type=F32,
    )
    squares[0] = tile

    barrier = pltpu.get_barrier_semaphore()
    for d in range(1, 16):
        pl.semaphore_signal(barrier, inc=1, device_id=seq_peer((s + d) % 16), device_id_type=MESH)
    for d in range(1, 8):
        pl.semaphore_signal(barrier, inc=1, device_id=tensor_peer((t + d) % 8), device_id_type=MESH)

    @pl.when(jnp.logical_not(own))
    def _():
        for c in range(2):
            pl.semaphore_signal(barrier, inc=1, device_id=(2 * t + c, i), device_id_type=MESH)

    pl.semaphore_wait(barrier, jnp.where(own, 22, 24))

    def remote(src, dst, send, recv, device):
        return pltpu.make_async_remote_copy(
            src_ref=src, dst_ref=dst, send_sem=send, recv_sem=recv, device_id=device, device_id_type=MESH
        )

    def exchange(count, src, dst, send, recv, peer):
        copies = [remote(src(d), dst(d), send.at[d], recv.at[d], peer(d)) for d in range(1, count)]
        for copy in copies:
            copy.start()
        return copies

    sq = exchange(8, lambda d: squares.at[0], lambda d: squares.at[d], sq_send, sq_recv, lambda d: tensor_peer((t + d) % 8))
    for copy in sq:
        copy.wait_recv()
    total = squares[0]
    for d in range(1, 8):
        total = total + squares[d]
    scale = lax.rsqrt(total / D + EPSILON)
    scale = jnp.transpose(jnp.broadcast_to(scale[0:1, :], (128, 128)))

    own_rows = pl.ds(pl.multiple_of(core * 128, 128), 128)
    quarter = index[0] % 4
    chosen = [jnp.zeros((128, 128), F32) for _ in range(4)]
    trace = jnp.zeros((128, 128), F32)
    for b in range(16):
        lanes = slice(b * 128, (b + 1) * 128)
        scaled = tok[:, lanes].astype(F32) * scale * gain[:, lanes]
        rounded = scaled.astype(BF16)
        cols[i, own_rows, lanes] = rounded
        wide = rounded.astype(F32)
        trace = trace + wide * wide
        chosen[b % 4] = chosen[b % 4] + jnp.where(quarter == b // 4, wide, 0.0)
        flipped[lanes, :] = (jnp.transpose(wide) * (1.0 / TOKENS)).astype(BF16)
    mine = jnp.where(index[0] // 4 == t, 1.0, 0.0)
    for b in range(4):
        masked[:, b * 128 : (b + 1) * 128] = (chosen[b] * mine).astype(BF16)
    trace_own[...] = jnp.sum(trace.reshape(16, 8, 128), axis=0)

    def piece_rows(k):
        return pl.ds(pl.multiple_of(k * 16, 16), 16)

    rs = exchange(
        8, lambda d: masked.at[piece_rows((t + d) % 8)], lambda d: sums.at[d], rs_send, rs_recv, lambda d: tensor_peer((t + d) % 8)
    )
    tt = exchange(8, lambda d: trace_own, lambda d: trace_t.at[d], tt_send, tt_recv, lambda d: tensor_peer((t + d) % 8))

    def flip_src(c):
        return flipped.at[pl.ds(c * 1024, 1024)]

    def flip_dst(c):
        return rows.at[i, :, pl.ds(pl.multiple_of(c * 128, 128), 128)]

    @pl.when(jnp.logical_not(own))
    def _():
        for c in range(2):
            remote(flip_src(c), flip_dst(core), x_send.at[c], x_recv.at[core], (2 * t + c, i)).start()

    own_half = pl.ds(pl.multiple_of(core * 1024, 1024), 1024)
    other_half = pl.ds(pl.multiple_of((1 - core) * 1024, 1024), 1024)

    @pl.when(own)
    def _():
        remote(flipped.at[other_half], flip_dst(core), x_send.at[0], x_recv.at[core], seq_peer(s + 1 - 2 * core)).start()
        pltpu.make_async_copy(flipped.at[own_half], flip_dst(core), x_local).start()

    for copy in rs:
        copy.wait_recv()
    total = masked[piece_rows(t), :].astype(F32)
    for d in range(1, 8):
        total = total + sums[d].astype(F32)

    def panel_piece(k):
        return panel.at[i, pl.ds(pl.multiple_of(core * 128 + k * 16, 16), 16), :]

    panel[i, pl.ds(pl.multiple_of(core * 128 + t * 16, 16), 16), :] = total.astype(BF16)
    ag = [
        remote(panel_piece(t), panel_piece(t), ag_send.at[d], ag_recv.at[d], tensor_peer((t + d) % 8)) for d in range(1, 8)
    ]
    for copy in ag:
        copy.start()
    for copy in tt:
        copy.wait_recv()
    total = trace_own[...]
    for d in range(1, 8):
        total = total + trace_t[d]
    trace_sum[...] = total
    ts = exchange(16, lambda d: trace_sum, lambda d: trace_s.at[d], ts_send, ts_recv, lambda d: seq_peer((s + d) % 16))

    class Ring:
        def __init__(self, slot, send, recv, partner, up, down, sibling):
            self.slot, self.send, self.recv = slot, send, recv
            self.peers = {"X": partner, "P": up, "M": down, "S": sibling}
            self.sent = []

        ITEMS = ("B", "A-", "A+", "B-", "B+", "A--", "B++", "SA", "SB", "SA-", "SA+", "SB-", "SB+", "SA--", "SB++")
        AT = {"A": (0, 0), "B": (0, 1), "A-": (-1, 0), "A+": (1, 0), "B-": (-1, 1), "B+": (1, 1), "A--": (-2, 0), "B++": (2, 1)}

        def copy(self, item, peer, lands):
            k = self.ITEMS.index(lands)
            ref = self.slot(*self.AT[item])
            return remote(ref, ref, self.send.at[k], self.recv.at[k], self.peers[peer])

        def go(self, item, *targets):
            for peer, lands in targets:
                self.copy(item, peer, lands).start()
                self.sent.append((item, peer, lands))
            if self.peers["S"] is not None:
                self.copy(item, "S", "S" + item).start()
                self.sent.append((item, "S", "S" + item))

        def wait(self, item):
            k = self.ITEMS.index(item)
            ref = self.slot(*self.AT[item], flip=False) if item[0] != "S" else self.slot(*self.AT[item[1:]], flip=True)
            remote(ref, ref, self.send.at[k], self.recv.at[k], self.peers["P"]).wait_recv()

        def step0(self):
            self.go("A", ("P", "A-"), ("M", "A+"), ("X", "B"))

        def step1(self):
            self.wait("B")
            self.go("B", ("P", "B-"), ("M", "B+"))

        def step2(self):
            self.wait("A-")
            self.go("A-", ("P", "A--"))
            self.wait("A+")
            self.go("A+")

        def step3(self):
            self.wait("B+")
            self.go("B+", ("M", "B++"))
            self.wait("B-")
            self.go("B-")

        def step4(self):
            self.wait("A--")
            self.go("A--")
            self.wait("B++")
            self.go("B++")

        def siblings(self, *items):
            for item in items:
                self.wait("S" + item)

        def drain(self):
            for sent in self.sent:
                self.copy(*sent).wait_send()

    def half_slot(buffer):
        def slot(dy, dx, flip=False):
            chunk = ((y + dy + 4) % 4) * 2 + (xl + dx) % 2
            half = (1 - core) if flip else core
            return buffer.at[chunk, pl.ds(pl.multiple_of(half * 128, 128), 128), :]
        return slot

    def row_slot(dz, dx, flip=False):
        return rows.at[((z + dz + 4) % 4) * 2 + (xh + dx) % 2]

    seq_ring = (seq_peer(s + 2 - 4 * xl), seq_peer((s + 4) % 16), seq_peer((s + 12) % 16), seq_peer(s + 1 - 2 * core))
    c_ring = Ring(half_slot(cols), c_send, c_recv, *seq_ring)
    p_ring = Ring(half_slot(panel), p_send, p_recv, *seq_ring)
    r_ring = Ring(row_slot, r_send, r_recv, tensor_peer(t + 1 - 2 * xh), tensor_peer((t + 2) % 8), tensor_peer((t + 6) % 8), None)

    for copy in (
        remote(panel_piece((t + 8 - d) % 8), panel_piece((t + 8 - d) % 8), ag_send.at[d], ag_recv.at[d], tensor_peer((t + d) % 8))
        for d in range(1, 8)
    ):
        copy.wait_recv()
    p_ring.step0()
    c_ring.step0()
    p_ring.step1()

    def flip_land(c):
        return rows.at[t, :, pl.ds(c * 128, 128)]

    for c in range(2):
        @pl.when(jnp.logical_not(jnp.logical_and(own, core == c)))
        def _():
            remote(flip_land(c), flip_land(c), x_send.at[0], x_recv.at[c], seq_peer(s + 1 - 2 * core)).wait_recv()

    @pl.when(own)
    def _():
        pltpu.make_async_copy(flipped.at[own_half], flip_dst(core), x_local).wait()

    r_ring.step0()
    p_ring.step2()
    p_ring.step3()
    p_ring.step4()
    c_ring.step1()
    p_ring.siblings("A", "B", "A-", "A+", "B-", "B+", "A--", "B++")
    r_ring.step1()

    for copy in ts:
        copy.wait_recv()
    total = trace_sum[...]
    for d in range(1, 16):
        total = total + trace_s[d]
    shift = DAMPING * (jnp.sum(total) / TOKENS) / D

    def fill(b, _):
        at = pl.ds(pl.multiple_of(b * 128, 128), 128)
        block = jnp.zeros((128, 512), F32)
        for k in range(8):
            block = block + dot(panel[k, :, at], panel[k], ((0,), (0,)))
        eye = (
            b * 128 + lax.broadcasted_iota(jnp.int32, (128, 512), 0)
            == lax.broadcasted_iota(jnp.int32, (128, 512), 1)
        )
        ext[at, 0:512] = block * (1.0 / TOKENS) + jnp.where(eye, shift, 0.0)
        ext[at, 512:1024] = jnp.where(eye, 1.0, 0.0)
        return 0

    lax.fori_loop(0, 4, fill, 0)

    def factor(b, _):
        base = b * 128
        at = pl.ds(pl.multiple_of(base, 128), 128)
        tiles = [ext[pl.ds(pl.multiple_of(base + 8 * g, 8), 8), at] for g in range(16)]
        inv = jnp.concatenate(inverse_factor(tiles), axis=0)
        upper = dot_split(inv, ext[at, :], ((1,), (0,)))
        inverse[at, :] = upper[:, 512:1024]
        for k in range(4):
            lanes = slice(k * 128, (k + 1) * 128)
            ext[lanes, :] = ext[lanes, :] - dot_split(upper[:, lanes], upper, ((0,), (0,)))

        return 0

    def gram_chunks(late):
        def body(k, _):
            ky = k // 2
            is_late = jnp.logical_or(ky == (y + 2) % 4, ky == jnp.where(y == z, (y + 3) % 4, (z + 2) % 4))
            @pl.when(is_late == late)
            def _():
                @pl.loop(0, 4)
                def _(m):
                    band = pl.ds(pl.multiple_of(m * 256, 256), 256)
                    for n in range(4):
                        lanes = slice(n * 512, (n + 1) * 512)
                        gram[band, lanes] += dot(rows[k, band, :], cols[k, :, lanes], ((1,), (0,)))
            return 0

        lax.fori_loop(0, 8, body, 0)

    @pl.loop(0, 8)
    def _(m):
        gram[pl.ds(pl.multiple_of(m * 128, 128), 128), :] = jnp.zeros((128, 2048), F32)

    def factor_and_forward(b, _):
        factor(b, 0)

        @pl.when(b == 0)
        def _():
            c_ring.step2()
            r_ring.step2()

        @pl.when(b == 2)
        def _():
            c_ring.step3()
            r_ring.step3()

        return 0

    lax.fori_loop(0, 4, factor_and_forward, 0)
    c_ring.siblings("A", "B", "A-", "A+", "B-", "B+")
    gram_chunks(False)
    r_ring.wait("A--")
    r_ring.wait("B++")

    @pl.loop(0, 8)
    def _(m):
        band = pl.ds(pl.multiple_of(m * 128, 128), 128)
        block = jnp.zeros((128, 512), F32)
        for k in range(8):
            block = block + dot(rows[k, band, :], panel[k], ((1,), (0,)))
        at = s * 1024 + m * 128 - start
        eye = at + lax.broadcasted_iota(jnp.int32, (128, 512), 0) == lax.broadcasted_iota(jnp.int32, (128, 512), 1)
        block = block + jnp.where(eye, shift, 0.0)
        white[band, :] = dot_split(block, inverse[...], ((1,), (1,))).astype(BF16)

    white_copy = pltpu.make_async_copy(white, panel_out, wh_sem)
    white_copy.start()
    for k in range(4):
        lanes = slice(k * 128, (k + 1) * 128)
        part[lanes, :] = dot(white[:, lanes], weight[...], ((0,), (1,)))

    def part_rows(k):
        return part.at[pl.ds(pl.multiple_of(k * 32, 32), 32)]

    fs = exchange(
        16, lambda d: part_rows((s + d) % 16), lambda d: landed.at[d], f_send, f_recv, lambda d: seq_peer((s + d) % 16)
    )
    c_ring.step4()
    c_ring.siblings("A--", "B++")
    gram_chunks(True)

    @pl.when(own)
    def _():
        @pl.loop(0, 8)
        def _(m):
            band = pl.ds(pl.multiple_of(m * 128, 128), 128)
            at = pl.ds(pl.multiple_of(core * 1024 + m * 128, 128), 128)
            eye = lax.broadcasted_iota(jnp.int32, (128, 128), 0) == lax.broadcasted_iota(jnp.int32, (128, 128), 1)
            gram[band, at] += jnp.where(eye, shift, 0.0)

    gram_copy = pltpu.make_async_copy(gram, gram_out, out_sem)
    gram_copy.start()
    for copy in fs:
        copy.wait_recv()
    total = part[pl.ds(pl.multiple_of(s * 32, 32), 32), :]
    for d in range(1, 16):
        total = total + landed[d]
    total = jnp.concatenate([total, jnp.zeros((96, 256), F32)], axis=0)
    proj_out[...] = jnp.transpose(total)[:, 0:32]

    for copies in (sq, rs, tt, ag, ts, fs):
        for copy in copies:
            copy.wait_send()
    for ring in (p_ring, c_ring, r_ring):
        ring.drain()
    remote(flipped.at[own_half], flip_dst(core), x_send.at[0], x_recv.at[0], seq_peer(s + 1 - 2 * core)).wait_send()

    @pl.when(jnp.logical_not(own))
    def _():
        remote(flipped.at[own_half], flip_dst(core), x_send.at[1], x_recv.at[0], seq_peer(s + 1 - 2 * core)).wait_send()

    white_copy.wait()
    gram_copy.wait()


def on_device(tokens, norm_gain, projection_weight, panel_index):
    vmem = pl.BlockSpec(memory_space=pltpu.VMEM)
    anywhere = pl.BlockSpec(memory_space=pl.ANY)
    dma = pltpu.SemaphoreType.DMA
    return pl.pallas_call(
        kernel,
        out_shape=(
            jax.ShapeDtypeStruct((1024, 2048), F32),
            jax.ShapeDtypeStruct((1024, 512), BF16),
            jax.ShapeDtypeStruct((256, 32), F32),
        ),
        in_specs=[vmem, vmem, pl.BlockSpec(memory_space=pltpu.SMEM), vmem],
        out_specs=(anywhere, anywhere, vmem),
        scratch_shapes=[
            pltpu.VMEM((8, 256, 2048), BF16),
            pltpu.VMEM((8, 1024, 256), BF16),
            pltpu.VMEM((8, 256, 512), BF16),
            pltpu.VMEM((1024, 2048), F32),
            pltpu.VMEM((512, 1024), F32),
            pltpu.VMEM((512, 512), F32),
            pltpu.VMEM((1024, 512), BF16),
            pltpu.VMEM((512, 256), F32),
            pltpu.VMEM((16, 32, 256), F32),
            pltpu.VMEM((2048, 128), BF16),
            pltpu.VMEM((8, 8, 128), F32),
            pltpu.VMEM((128, 512), BF16),
            pltpu.VMEM((8, 16, 512), BF16),
            pltpu.VMEM((8, 128), F32),
            pltpu.VMEM((8, 8, 128), F32),
            pltpu.VMEM((16, 8, 128), F32),
            pltpu.VMEM((8, 128), F32),
            dma((8,)), dma((8,)), dma((8,)), dma((8,)), dma((8,)), dma((8,)), dma((8,)), dma((8,)), dma((16,)), dma((16,)),
            dma((15,)), dma((15,)), dma((15,)), dma((15,)), dma((15,)), dma((15,)), dma((2,)), dma((2,)), dma,
            dma((16,)), dma((16,)), dma, dma,
        ],
        compiler_params=pltpu.CompilerParams(
            collective_id=0, has_side_effects=True, vmem_limit_bytes=50 * 1024 * 1024
        ),
        cost_estimate=pl.CostEstimate(flops=12_000_000_000, bytes_accessed=20_000_000, transcendentals=0),
        name="whiten",
    )(tokens, norm_gain[None, :], panel_index, projection_weight)


def solution(mesh):
    placed = (P("seq", "tensor"), P("tensor"), P("tensor", "seq"), P())
    return jax.shard_map(
        on_device,
        mesh=mesh,
        in_specs=placed,
        out_specs=(P("seq", "tensor"), P("seq", None), P("tensor", "seq")),
        check_vma=False,
    )
```

time: 749 us -> 143 us (0.19); the launches traced: 739 us -> 143 us
  waiting for transfers between devices: 306 us -> 0 us
  blocking collectives: 232 us -> 0 us
  other arithmetic: 132 us -> 0 us
  Pallas kernels: 0 us -> 129 us
  matrix products: 27 us -> 0 us
  between operations: 18.2 us -> 1.3 us
  local copies, waits for them, and re-layouts: 24.1 us -> 12.3 us
    psum x2 -> x0, blocking collectives: 232 us -> none  [the longest x1 209 us: on_device(): lax.psum(jnp.sum(normed_wide * normed_wide), ('seq', 'tensor')) / tokens_all]
    psum x3 -> x0, waiting for transfers between devices: 203 us -> none  [broadcast(): return lax.psum(kept, axis)]
    pallas_call x0 -> x1, Pallas kernels: none -> 129 us  [on_device(): pl.pallas_call(kernel, out_shape=(jax.ShapeDtypeStruct((1024, 2048), F32)...]
    another operation x17 -> x0, other arithmetic: 118 us -> none  [the longest x14 78.6 us: on_device(): factor = jnp.linalg.cholesky(diag_block)]
    all_gather x1 -> x0, waiting for transfers between devices: 52.8 us -> none  [on_device(): columns = lax.all_gather(normed, 'seq', axis=0, tiled=True)]
    reduce_scatter x1 -> x0, waiting for transfers between devices: 50 us -> none  [on_device(): lax.psum_scatter(partial_value, 'seq', scatter_dimension=1, tiled=True)]
    dot_general x2 -> x0, matrix products: 15.5 us -> none  [the longest x1 13 us: on_device(): lax.dot_general(row_part, columns, (((0,), (0,)), ((), ())), preferred_el...]
    another operation x13 -> x0, matrix products: 11.5 us -> none  [the longest x7 9.18 us: on_device(): lax.linalg.triangular_solve(factor, panel_rows, left_side=False, lower=Tr...]
  transfers between devices with their start and end apart: 5 -> 0, of which waited for: 4 -> 0; matrix products, arithmetic and copies ran while one was open for 1% -> 0% of each run, Pallas kernels for 0% -> 0%
where the time goes in v1:
time: 143 us
  Pallas kernels  129 us (90%)
  local copies, waits for them, and re-layouts  12.3 us (9%)
    pallas_call x1, Pallas kernels, on_device(): pl.pallas_call(kernel, out_shape=(jax.ShapeDtypeStruct((1024, 2048), F32)...  129 us
    unnamed x8, local copies, waits for them, and re-layouts  11.6 us

profile of v1, /device:TPU:1, one launch (start us, length us, event | category | flops | bytes accessed | tf_op | source)
XLA Modules:
  0.0 142.5 jit_solution(17911521600048853425)
XLA Ops:
  1.3 0.0 copy-start
  1.3 1.0 copy-done
  2.3 0.0 copy-start.1
  2.3 1.0 copy-done.1
  3.4 0.0 copy-start.2
  3.4 0.7 copy-done.2
  4.1 128.9 %whiten.1 = (f32[1024,2048]{1,0:T(8,128)}, bf16[1024,512]{1,0:T(8,128)(2,1)S(1)}, f32[256,32]{1,0:T(8,128)S(1)}) custom-call(bf16[128,2048]{1,0:T(8,128)(2,1)S(1)} %copy-done, f32[1,2048]{1,0:T(1,128)S(1)} %bitcast.1, s32[1]{0:T(128)S(6)} %copy.10.index, bf16[256,1024]{1,0:T(8,128)(2,1)S(1)} %copy-done.1), custom_call_target="tpu_custom_call" | custom-call | flops 12000000000 | bytes 20000000 | tf_op jit(solution)/shard_map/whiten/pallas_call | solution.py:445
  133.0 0.7 copy.7
  133.7 7.9 %copy.11 = f32[1024,2048]{1,0:T(8,128)} copy(f32[1024,2048]{1,0:T(8,128)} %get-tuple-element.9) | data formatting | bytes 16777216
  141.5 1.0 copy.12
Async XLA Ops:
  1.3 1.0 copy-start
  2.3 1.0 copy-start.1
  3.4 0.7 copy-start.2

commit v2 on v1

v2 whole, which is shorter than its diff:
```python
import functools

import jax
import jax.numpy as jnp
from jax import lax
from jax.experimental import pallas as pl
from jax.experimental.pallas import tpu as pltpu
from jax.sharding import PartitionSpec as P

D = 16384
PANEL = 512
TOKENS = 2048
EPSILON = 1e-05
DAMPING = 0.1
F32 = jnp.float32
BF16 = jnp.bfloat16
MESH = pl.DeviceIdType.MESH


def halves(a):
    high = a.astype(BF16)
    return high, (a - high.astype(F32)).astype(BF16)


def dot(a, b, dims):
    return lax.dot_general(a, b, (dims, ((), ())), preferred_element_type=F32)


def dot_split(a, b, dims):
    ah, al = halves(a)
    bh, bl = halves(b)
    return dot(ah, bh, dims) + (dot(ah, bl, dims) + dot(al, bh, dims))


def row_of(tile, r):
    return jnp.broadcast_to(tile[r : r + 1, :], (8, 128))


def column_of(tile, k):
    return jnp.broadcast_to(tile[:, k : k + 1], (8, 128))


def inverse_factor(a):
    sub = lax.broadcasted_iota(jnp.int32, (8, 128), 0)
    lane = lax.broadcasted_iota(jnp.int32, (8, 128), 1)
    inv = [jnp.where(sub + 8 * g == lane, 1.0, 0.0).astype(F32) for g in range(16)]
    for g in range(16):
        cols = [{k: column_of(a[k], 8 * g + c) for k in range(g, 16)} for c in range(8)]
        for c in range(8):
            r = lax.rsqrt(row_of(cols[c][g], c))
            m = {k: cols[c][k] * r for k in range(g, 16)}
            for c2 in range(c + 1, 8):
                f = row_of(cols[c2][g], c) * r
                for k in range(g, 16):
                    cols[c2][k] = cols[c2][k] - m[k] * f
            u = row_of(a[g], c) * r
            z = row_of(inv[g], c) * r
            m[g] = jnp.where(sub > c, m[g], 0.0)
            for k in range(g, 16):
                a[k] = a[k] - m[k] * u
                inv[k] = inv[k] - m[k] * z
            inv[g] = jnp.where(sub == c, z, inv[g])
    return inv


def kernel(
    tok_hbm, gain_hbm, index, weight_hbm,
    gram, white, proj_out,
    tok, gain, weight, cols, rows, panel, ext, inverse, part, landed,
    flipped, squares, masked, sums, gain_own, gain_t, scales, trace_own, trace_t, trace_s, trace_sum,
    in_sem, sq_send, sq_recv, rs_send, rs_recv, gt_send, gt_recv, ag_send, ag_recv, tt_send, tt_recv, ts_send, ts_recv,
    p_send, p_recv, c_send, c_recv, r_send, r_recv, x_send, x_recv, x_local, y_send, y_recv, relay, gain_far, scale_lanes, right, f_send, f_recv,
):
    s, t = lax.axis_index("seq"), lax.axis_index("tensor")
    i, core = s // 2, s % 2
    y, xl = i // 2, i % 2
    z, xh = t // 2, t % 2
    start = index[0] * PANEL
    first = ((z + 4 - y) % 4) * 2 + xh
    mirror = 2 * z + xl
    shifted = ((z + y) % 4) * 2 + xh
    own = jnp.logical_and(first == i, mirror == t)

    def seq_peer(k):
        return (k, t)

    def tensor_peer(k):
        return (s, k)

    fetch = [
        pltpu.make_async_copy(tok_hbm, tok, in_sem.at[0]),
        pltpu.make_async_copy(gain_hbm, gain, in_sem.at[1]),
        pltpu.make_async_copy(weight_hbm, weight, in_sem.at[2]),
    ]
    for copy in fetch:
        copy.start()

    barrier = pltpu.get_barrier_semaphore()
    for d in range(1, 16):
        pl.semaphore_signal(barrier, inc=1, device_id=seq_peer((s + d) % 16), device_id_type=MESH)
    for d in range(1, 8):
        pl.semaphore_signal(barrier, inc=1, device_id=tensor_peer((t + d) % 8), device_id_type=MESH)

    @pl.when(xl != xh)
    def _():
        for c in range(2):
            pl.semaphore_signal(barrier, inc=1, device_id=(2 * first + c, mirror), device_id_type=MESH)

    fetch[0].wait()
    fetch[1].wait()
    quarter = index[0] % 4
    mine = index[0] // 4 == t
    chosen = [jnp.zeros((128, 128), F32) for _ in range(4)]
    part_sq = jnp.zeros((128, 128), F32)
    for b in range(16):
        piece = tok[:, b * 128 : (b + 1) * 128].astype(F32)
        part_sq = part_sq + piece * piece
        flipped[b * 128 : (b + 1) * 128, :] = jnp.transpose(piece).astype(BF16)
        taken = jnp.logical_and(mine, quarter == b // 4)
        chosen[b % 4] = chosen[b % 4] + jnp.where(taken, piece, 0.0)
    for b in range(4):
        masked[:, b * 128 : (b + 1) * 128] = chosen[b].astype(BF16)
    taken = jnp.zeros((1, 512), F32)
    for b in range(4):
        taken = taken + jnp.where(jnp.logical_and(mine, quarter == b), gain[:, b * 512 : (b + 1) * 512], 0.0)
    gain_own[...] = jnp.broadcast_to(taken, (8, 512))
    squares[0] = lax.dot_general(
        jnp.ones((8, 128), F32), part_sq, (((1,), (1,)), ((), ())),
        precision=lax.Precision.HIGHEST, preferred_element_type=F32,
    )

    pl.semaphore_wait(barrier, jnp.where(xl == xh, 22, 24))

    def remote(src, dst, send, recv, device):
        return pltpu.make_async_remote_copy(
            src_ref=src, dst_ref=dst, send_sem=send, recv_sem=recv, device_id=device, device_id_type=MESH
        )

    def exchange(count, src, dst, send, recv, peer):
        copies = [remote(src(d), dst(d), send.at[d], recv.at[d], peer(d)) for d in range(1, count)]
        for copy in copies:
            copy.start()
        return copies

    def piece_rows(k):
        return pl.ds(pl.multiple_of(k * 16, 16), 16)

    def across(d):
        return tensor_peer((t + d) % 8)

    def along(d):
        return seq_peer((s + d) % 16)

    sq = exchange(8, lambda d: squares.at[0], lambda d: squares.at[d], sq_send, sq_recv, across)
    rs = exchange(8, lambda d: masked.at[piece_rows((t + d) % 8)], lambda d: sums.at[d], rs_send, rs_recv, across)
    gt = exchange(8, lambda d: gain_own, lambda d: gain_t.at[d], gt_send, gt_recv, across)
    def quarter_of(src, c, q):
        return src.at[pl.ds(c * 1024 + q * 512, 512)]

    def landing(chunk, c, q):
        return rows.at[chunk, c, pl.ds(q * 512, 512)]

    def into_rows(c, q, src):
        sem = 2 * q + c
        return remote(
            quarter_of(src, c, q), landing(i, core, q), x_send.at[sem], x_recv.at[2 * q + core], (2 * first + c, mirror)
        )

    def to_shifted(c, q):
        sem = 2 * q + c
        return remote(quarter_of(flipped, c, q), quarter_of(relay, c, q), y_send.at[sem], y_recv.at[sem], tensor_peer(shifted))

    def gain_to_shifted():
        return remote(gain, gain_far, y_send.at[4], y_recv.at[4], tensor_peer(shifted))

    def shift_start(q):
        @pl.when(y != 0)
        def _():
            if q == 0:
                gain_to_shifted().start()
            else:
                for c in range(2):
                    to_shifted(c, 0).wait_send()
            for c in range(2):
                to_shifted(c, q).start()

    def to_mirror(src, gains, q):
        for c in range(2):
            @pl.loop(0, 4)
            def _(b):
                at = pl.ds(pl.multiple_of(c * 1024 + q * 512 + b * 128, 128), 128)
                by_row = jnp.transpose(jnp.broadcast_to(gains[:, at], (128, 128)))
                by_lane = jnp.broadcast_to(scale_lanes[0:1, :], (128, 128))
                src[at, :] = (src[at, :].astype(F32) * by_lane * by_row * (1.0 / TOKENS)).astype(BF16)

            keeps = jnp.logical_and(own, core == c)

            @pl.when(keeps)
            def _():
                pltpu.make_async_copy(quarter_of(src, c, q), landing(i, core, q), x_local.at[q]).start()

            @pl.when(jnp.logical_not(keeps))
            def _():
                into_rows(c, q, src).start()

    def relay_on(q):
        @pl.when(y == 0)
        def _():
            to_mirror(flipped, gain, q)

        @pl.when(y != 0)
        def _():
            if q == 0:
                gain_to_shifted().wait_recv()
            for c in range(2):
                to_shifted(c, q).wait_recv()
            to_mirror(relay, gain_far, q)

    def landed_rows(q):
        for c in range(2):
            @pl.when(jnp.logical_not(jnp.logical_and(own, core == c)))
            def _():
                there = landing(first, c, q)
                remote(there, there, x_send.at[0], x_recv.at[2 * q + c], seq_peer(s + 1 - 2 * core)).wait_recv()

        @pl.when(own)
        def _():
            pltpu.make_async_copy(quarter_of(flipped, 0, q), landing(i, core, q), x_local.at[q]).wait()

    shift_start(0)
    for copy in sq:
        copy.wait_recv()
    total = squares[0]
    for d in range(1, 8):
        total = total + squares[d]
    scale = lax.rsqrt(total / D + EPSILON)
    scale_lanes[...] = scale
    scale = jnp.transpose(jnp.broadcast_to(scale[0:1, :], (128, 128)))
    scales[...] = scale
    shift_start(1)

    for copy in rs + gt:
        copy.wait_recv()
    total = masked[piece_rows(t), :].astype(F32)
    total_gain = gain_own[0:1, :]
    for d in range(1, 8):
        total = total + sums[d].astype(F32)
        total_gain = total_gain + gain_t[d, 0:1, :]

    def panel_piece(k):
        return panel.at[i, pl.ds(pl.multiple_of(core * 128 + k * 16, 16), 16), :]

    piece_scale = scales[piece_rows(t), :]
    for b in range(4):
        lanes = slice(b * 128, (b + 1) * 128)
        panel[i, pl.ds(pl.multiple_of(core * 128 + t * 16, 16), 16), lanes] = (
            total[:, lanes] * piece_scale * total_gain[:, lanes]
        ).astype(BF16)
    ag = [remote(panel_piece(t), panel_piece(t), ag_send.at[d], ag_recv.at[d], across(d)) for d in range(1, 8)]
    for copy in ag:
        copy.start()

    relay_on(0)
    own_rows = pl.ds(pl.multiple_of(core * 128, 128), 128)
    trace = jnp.zeros((128, 128), F32)
    for b in range(16):
        lanes = slice(b * 128, (b + 1) * 128)
        scaled = tok[:, lanes].astype(F32) * scale * gain[:, lanes]
        rounded = scaled.astype(BF16)
        cols[i, own_rows, lanes] = rounded
        wide = rounded.astype(F32)
        trace = trace + wide * wide
    trace_own[...] = jnp.sum(trace.reshape(16, 8, 128), axis=0)
    tt = exchange(8, lambda d: trace_own, lambda d: trace_t.at[d], tt_send, tt_recv, across)

    class Ring:
        ITEMS = ("B", "A-", "A+", "B-", "B+", "A--", "B++", "C-", "C+", "C--")
        AT = {
            "A": (0, 0), "B": (0, 1), "A-": (-1, 0), "A+": (1, 0), "B-": (-1, 1), "B+": (1, 1), "A--": (-2, 0), "B++": (2, 1),
            "C-": (-1, 1), "C+": (1, 1), "C--": (2, 1),
        }

        def __init__(self, slot, send, recv, partner, up, down, sibling, split=None):
            self.slot, self.send, self.recv, self.split = slot, send, recv, split
            self.peers = {"X": partner, "P": up, "M": down, "S": sibling}
            self.sent = []

        def part(self, kind):
            if self.split is None:
                return None
            return {"A": None, "B": (0, self.split), "C": (self.split, 128)}[kind]

        def copy(self, item, peer, lands):
            k = (11 if lands[0] == "S" else 0) + (("A",) + self.ITEMS).index(lands.lstrip("S"))
            kind = lands.lstrip("S")[0]
            ref = self.slot(*self.AT[item], rows=None if lands.lstrip("S") == "B" else self.part(kind))
            return remote(ref, ref, self.send.at[k], self.recv.at[k], self.peers[peer])

        def go(self, item, *targets):
            if self.peers["S"] is not None:
                targets = targets + (("S", "S" + item),)
            for peer, lands in targets:
                self.copy(item, peer, lands).start()
                self.sent.append((item, peer, lands))

        def wait(self, item):
            k = (11 if item[0] == "S" else 0) + (("A",) + self.ITEMS).index(item.lstrip("S"))
            name = item.lstrip("S")
            ref = self.slot(*self.AT[name], flip=item[0] == "S", rows=None if name == "B" else self.part(name[0]))
            remote(ref, ref, self.send.at[k], self.recv.at[k], self.peers["P"]).wait_recv()

        def across(self, lands):
            return () if self.split is None else (("X", lands),)

        def step0(self):
            self.go("A", ("P", "A-"), ("M", "A+"), ("X", "B"))

        def step1(self):
            self.wait("B")
            self.go("B", ("P", "B-"), ("M", "B+"))

        def step2(self):
            self.wait("A-")
            self.go("A-", ("P", "A--"), *self.across("C-"))
            self.wait("A+")
            self.go("A+", *self.across("C+"))

        def step3(self):
            self.wait("B+")
            self.go("B+", ("M", "B++"))
            self.wait("B-")
            self.go("B-")
            if self.split is not None:
                self.wait("C-")
                self.go("C-")
                self.wait("C+")
                self.go("C+")

        def step4(self):
            self.wait("A--")
            self.go("A--", *self.across("C--"))
            self.wait("B++")
            self.go("B++")

        def step5(self):
            self.wait("C--")
            self.go("C--")

        def siblings(self, *items):
            for item in items:
                self.wait("S" + item)

        def drain(self):
            for sent in self.sent:
                self.copy(*sent).wait_send()

    def half_slot(buffer):
        def slot(dy, dx, flip=False, rows=None):
            low, high = rows or (0, 128)
            chunk = ((y + dy + 4) % 4) * 2 + (xl + dx) % 2
            half = (1 - core) if flip else core
            return buffer.at[chunk, pl.ds(pl.multiple_of(half * 128 + low, 16), high - low), :]
        return slot

    def row_slot(dz, dx, **_):
        return rows.at[((z + 8 + dz - y) % 4) * 2 + (xh + dx) % 2]

    def row_part(q):
        return lambda dz, dx, **_: row_slot(dz, dx).at[:, pl.ds(q * 512, 512)]

    seq_ring = (seq_peer(s + 2 - 4 * xl), seq_peer((s + 4) % 16), seq_peer((s + 12) % 16), seq_peer(s + 1 - 2 * core))
    c_ring = Ring(half_slot(cols), c_send, c_recv, *seq_ring, split=80)
    p_ring = Ring(half_slot(panel), p_send, p_recv, *seq_ring)
    z_ring = (tensor_peer(t + 1 - 2 * xh), tensor_peer((t + 2) % 8), tensor_peer((t + 6) % 8), None)
    r_ring = [Ring(row_part(q), r_send.at[q], r_recv.at[q], *z_ring) for q in range(2)]

    for d in range(1, 8):
        there = panel_piece((t + 8 - d) % 8)
        remote(there, there, ag_send.at[d], ag_recv.at[d], across(d)).wait_recv()
    p_ring.step0()

    for copy in tt:
        copy.wait_recv()
    total = trace_own[...]
    for d in range(1, 8):
        total = total + trace_t[d]
    trace_sum[...] = total
    ts = exchange(16, lambda d: trace_sum, lambda d: trace_s.at[d], ts_send, ts_recv, along)
    p_ring.step1()
    relay_on(1)
    p_ring.step2()
    p_ring.step3()
    c_ring.step0()
    landed_rows(0)
    r_ring[0].step0()
    p_ring.step4()
    p_ring.siblings("A", "B", "A-", "A+", "B-", "B+", "A--", "B++")

    for copy in ts:
        copy.wait_recv()
    total = trace_sum[...]
    for d in range(1, 16):
        total = total + trace_s[d]
    shift = DAMPING * (jnp.sum(total) / TOKENS) / D

    def fill(b, _):
        at = pl.ds(pl.multiple_of(b * 128, 128), 128)
        block = jnp.zeros((128, 512), F32)
        for k in range(8):
            block = block + dot(panel[k, :, at], panel[k], ((0,), (0,)))
        eye = (
            b * 128 + lax.broadcasted_iota(jnp.int32, (128, 512), 0)
            == lax.broadcasted_iota(jnp.int32, (128, 512), 1)
        )
        ext[at, 0:512] = block * (1.0 / TOKENS) + jnp.where(eye, shift, 0.0)
        ext[at, 512:1024] = jnp.where(eye, 1.0, 0.0)
        return 0

    lax.fori_loop(0, 4, fill, 0)
    landed_rows(1)
    r_ring[1].step0()
    c_ring.step1()

    far = (y + 2) % 4
    apart = (z + 8 - 2 * y) % 4
    early = [(far + jnp.where(apart >= 2, 1, 2)) % 4, (far + jnp.where(apart == 3, 2, 3)) % 4]
    late = [far, (far + jnp.where(apart == 0, 1, apart)) % 4]

    def row_band(k, band):
        return jnp.concatenate([rows[k, 0, band, :], rows[k, 1, band, :]], axis=1)

    def product(chunks, band, right_of):
        total = None
        for ky in chunks:
            for kx in range(2):
                k = ky * 2 + kx
                term = dot(row_band(k, band), right_of(k), ((1,), (0,)))
                total = term if total is None else total + term
        return total

    def gram_band(chunks, band):
        for n in range(4):
            lanes = slice(n * 512, (n + 1) * 512)
            yield lanes, product(chunks, band, lambda k: cols[k, :, lanes])

    def factor(b):
        base = b * 128
        at = pl.ds(pl.multiple_of(base, 128), 128)
        tiles = [ext[pl.ds(pl.multiple_of(base + 8 * g, 8), 8), at] for g in range(16)]
        inv = jnp.concatenate(inverse_factor(tiles), axis=0)
        upper = dot_split(inv, ext[at, :], ((1,), (0,)))
        inverse[at, :] = upper[:, 512:1024]
        for k in range(4):
            lanes = slice(k * 128, (k + 1) * 128)
            ext[lanes, :] = ext[lanes, :] - dot_split(upper[:, lanes], upper, ((0,), (0,)))

    def factor_and_forward(b, _):
        factor(b)

        @pl.when(b == 0)
        def _():
            r_ring[0].step1()
            c_ring.step2()
            r_ring[0].step2()

        @pl.when(b == 1)
        def _():
            r_ring[1].step1()
            c_ring.step3()
            r_ring[1].step2()

        @pl.when(b == 2)
        def _():
            r_ring[0].step3()
            r_ring[1].step3()
            c_ring.step4()

        @pl.when(b == 3)
        def _():
            c_ring.step5()

        return 0

    lax.fori_loop(0, 4, factor_and_forward, 0)
    c_ring.siblings("A", "B", "A-", "A+", "B-", "B+", "C-", "C+")

    @pl.loop(0, 8)
    def _(m):
        band = pl.ds(pl.multiple_of(m * 128, 128), 128)
        right[band, :] = product(early, band, lambda k: panel[k])
        for lanes, value in gram_band(early, band):
            gram[band, lanes] = value

    for ring in r_ring:
        ring.wait("A--")
        ring.wait("B++")

    @pl.loop(0, 8)
    def _(m):
        band = pl.ds(pl.multiple_of(m * 128, 128), 128)
        at = s * 1024 + m * 128 - start
        eye = at + lax.broadcasted_iota(jnp.int32, (128, 512), 0) == lax.broadcasted_iota(jnp.int32, (128, 512), 1)
        block = right[band, :] + product(late, band, lambda k: panel[k]) + jnp.where(eye, shift, 0.0)
        white[band, :] = dot_split(block, inverse[...], ((1,), (1,))).astype(BF16)

    fetch[2].wait()
    for k in range(4):
        lanes = slice(k * 128, (k + 1) * 128)
        part[lanes, :] = dot(white[:, lanes], weight[...], ((0,), (1,)))

    def part_rows(k):
        return part.at[pl.ds(pl.multiple_of(k * 32, 32), 32)]

    fs = exchange(16, lambda d: part_rows((s + d) % 16), lambda d: landed.at[d], f_send, f_recv, along)
    c_ring.siblings("A--", "B++", "C--")

    @pl.loop(0, 8)
    def _(m):
        band = pl.ds(pl.multiple_of(m * 128, 128), 128)
        for lanes, value in gram_band(late, band):
            gram[band, lanes] = gram[band, lanes] + value

    @pl.when(i == t)
    def _():
        @pl.loop(0, 8)
        def _(m):
            band = pl.ds(pl.multiple_of(m * 128, 128), 128)
            at = pl.ds(pl.multiple_of(core * 1024 + m * 128, 128), 128)
            eye = lax.broadcasted_iota(jnp.int32, (128, 128), 0) == lax.broadcasted_iota(jnp.int32, (128, 128), 1)
            gram[band, at] += jnp.where(eye, shift, 0.0)

    for copy in fs:
        copy.wait_recv()
    total = part[pl.ds(pl.multiple_of(s * 32, 32), 32), :]
    for d in range(1, 16):
        total = total + landed[d]
    proj_out[...] = total

    for copies in (sq, rs, gt, tt, ag, ts, fs):
        for copy in copies:
            copy.wait_send()
    for ring in (p_ring, c_ring, *r_ring):
        ring.drain()
    for c in range(2):
        @pl.when(jnp.logical_not(jnp.logical_and(own, core == c)))
        def _():
            for q in range(2):
                into_rows(c, q, flipped).wait_send()

        @pl.when(y != 0)
        def _():
            to_shifted(c, 1).wait_send()

    @pl.when(y != 0)
    def _():
        gain_to_shifted().wait_send()


def on_device(tokens, norm_gain, projection_weight, panel_index):
    vmem = pl.BlockSpec(memory_space=pltpu.VMEM)
    hbm = pl.BlockSpec(memory_space=pltpu.HBM)
    dma = pltpu.SemaphoreType.DMA
    gram, white, projected = pl.pallas_call(
        kernel,
        out_shape=(
            jax.ShapeDtypeStruct((1024, 2048), F32),
            jax.ShapeDtypeStruct((1024, 512), BF16),
            jax.ShapeDtypeStruct((32, 256), F32),
        ),
        in_specs=[hbm, hbm, pl.BlockSpec(memory_space=pltpu.SMEM), hbm],
        out_specs=(vmem, vmem, vmem),
        scratch_shapes=[
            pltpu.VMEM((128, 2048), BF16),
            pltpu.VMEM((1, 2048), F32),
            pltpu.VMEM((256, 1024), BF16),
            pltpu.VMEM((8, 256, 2048), BF16),
            pltpu.VMEM((8, 2, 1024, 128), BF16),
            pltpu.VMEM((8, 256, 512), BF16),
            pltpu.VMEM((512, 1024), F32),
            pltpu.VMEM((512, 512), F32),
            pltpu.VMEM((512, 256), F32),
            pltpu.VMEM((16, 32, 256), F32),
            pltpu.VMEM((2048, 128), BF16),
            pltpu.VMEM((8, 8, 128), F32),
            pltpu.VMEM((128, 512), BF16),
            pltpu.VMEM((8, 16, 512), BF16),
            pltpu.VMEM((8, 512), F32),
            pltpu.VMEM((8, 8, 512), F32),
            pltpu.VMEM((128, 128), F32),
            pltpu.VMEM((8, 128), F32),
            pltpu.VMEM((8, 8, 128), F32),
            pltpu.VMEM((16, 8, 128), F32),
            pltpu.VMEM((8, 128), F32),
            dma((3,)),
            dma((8,)), dma((8,)), dma((8,)), dma((8,)), dma((8,)), dma((8,)),
            dma((8,)), dma((8,)), dma((8,)), dma((8,)), dma((16,)), dma((16,)),
            dma((22,)), dma((22,)), dma((22,)), dma((22,)), dma((2, 22)), dma((2, 22)), dma((4,)), dma((4,)), dma((2,)), dma((5,)), dma((5,)),
            pltpu.VMEM((2048, 128), BF16), pltpu.VMEM((1, 2048), F32), pltpu.VMEM((8, 128), F32),
            pltpu.VMEM((1024, 512), F32), dma((16,)), dma((16,)),
        ],
        compiler_params=pltpu.CompilerParams(
            collective_id=0, has_side_effects=True, vmem_limit_bytes=36 * 1024 * 1024
        ),
        cost_estimate=pl.CostEstimate(flops=12_000_000_000, bytes_accessed=20_000_000, transcendentals=0),
        name="whiten",
    )(tokens, norm_gain[None, :], panel_index, projection_weight)
    return gram, white, projected.T


def solution(mesh):
    placed = (P("seq", "tensor"), P("tensor"), P("tensor", "seq"), P())
    return jax.shard_map(
        on_device,
        mesh=mesh,
        in_specs=placed,
        out_specs=(P("seq", "tensor"), P("seq", None), P("tensor", "seq")),
        check_vma=False,
    )
```

time: 143 us -> 119 us (0.83)
  Pallas kernels: 129 us -> 109 us
  local copies, waits for them, and re-layouts: 12.3 us -> 7.76 us
    pallas_call x1, Pallas kernels: 129 us -> 109 us  [on_device(): pl.pallas_call(kernel, out_shape=(jax.ShapeDtypeStruct((1024, 2048), F32)...]
    unnamed x8 -> x9, local copies, waits for them, and re-layouts: 11.6 us -> 7.76 us
where the time goes in v2:
time: 119 us; the launch traced here: 118 us
  Pallas kernels  109 us (92%)
  local copies, waits for them, and re-layouts  7.76 us (7%)
  between operations  1.3 us (1%)
    pallas_call x1, Pallas kernels, on_device(): pl.pallas_call(kernel, out_shape=(jax.ShapeDtypeStruct((1024, 2048), F32)...  109 us
    unnamed x9, local copies, waits for them, and re-layouts  7.76 us

profile of v2, /device:TPU:1, one launch (start us, length us, event | category | flops | bytes accessed | tf_op | source)
XLA Modules:
  0.0 118.0 jit_solution(635520235787431607)
XLA Ops:
  1.3 0.0 copy-start
  1.3 1.0 copy-done
  2.3 0.0 copy-start.1
  2.3 1.0 copy-done.1
  3.4 0.0 copy-start.2
  3.4 0.7 copy-done.2
  4.1 108.9 %whiten.1 = (f32[1024,2048]{1,0:T(8,128)S(1)}, bf16[1024,512]{1,0:T(8,128)(2,1)S(1)}, f32[32,256]{1,0:T(8,128)S(1)}) custom-call(bf16[128,2048]{1,0:T(8,128)(2,1)S(1)} %copy-done, f32[1,2048]{1,0:T(1,128)S(1)} %bitcast.3, s32[1]{0:T(128)S(6)} %copy.10.index, bf16[256,1024]{1,0:T(8,128)(2,1)S(1)} %copy-done.1), custom_call_target="tpu_custom_call" | custom-call | flops 12000000000 | bytes 20000000 | tf_op jit(solution)/shard_map/whiten/pallas_call | solution.py:563
  113.0 3.4 %copy.11 = f32[1024,2048]{1,0:T(8,128)} copy(f32[1024,2048]{1,0:T(8,128)S(1)} %get-tuple-element.12) | data formatting | bytes 16777216
  116.4 1.0 copy.12
  117.4 0.6 copy.13
Async XLA Ops:
  1.3 1.0 copy-start
  2.3 1.0 copy-start.1
  3.4 0.7 copy-start.2

commit v3 on v2

--- a/solution.py
+++ b/solution.py
@@ -12,6 +12,7 @@
 TOKENS = 2048
 EPSILON = 1e-05
 DAMPING = 0.1
+BAND = 512
 F32 = jnp.float32
 BF16 = jnp.bfloat16
 MESH = pl.DeviceIdType.MESH
@@ -69,7 +70,7 @@
     tok, gain, weight, cols, rows, panel, ext, inverse, part, landed,
     flipped, squares, masked, sums, gain_own, gain_t, scales, trace_own, trace_t, trace_s, trace_sum,
     in_sem, sq_send, sq_recv, rs_send, rs_recv, gt_send, gt_recv, ag_send, ag_recv, tt_send, tt_recv, ts_send, ts_recv,
-    p_send, p_recv, c_send, c_recv, r_send, r_recv, x_send, x_recv, x_local, y_send, y_recv, relay, gain_far, scale_lanes, right, f_send, f_recv,
+    p_send, p_recv, c_send, c_recv, r_send, r_recv, x_send, x_recv, x_local, y_send, y_recv, relay, gain_far, scale_lanes, right, above, f_send, f_recv,
 ):
     s, t = lax.axis_index("seq"), lax.axis_index("tensor")
     i, core = s // 2, s % 2
@@ -450,9 +451,14 @@
         inv = jnp.concatenate(inverse_factor(tiles), axis=0)
         upper = dot_split(inv, ext[at, :], ((1,), (0,)))
         inverse[at, :] = upper[:, 512:1024]
-        for k in range(4):
-            lanes = slice(k * 128, (k + 1) * 128)
-            ext[lanes, :] = ext[lanes, :] - dot_split(upper[:, lanes], upper, ((0,), (0,)))
+        above[...] = upper
+
+        def below(k, _):
+            lanes = pl.ds(pl.multiple_of(k * 128, 128), 128)
+            ext[lanes, :] = ext[lanes, :] - dot_split(above[:, lanes], above[...], ((0,), (0,)))
+            return 0
+
+        lax.fori_loop(b + 1, 4, below, 0)
 
     def factor_and_forward(b, _):
         factor(b)
@@ -484,9 +490,9 @@
     lax.fori_loop(0, 4, factor_and_forward, 0)
     c_ring.siblings("A", "B", "A-", "A+", "B-", "B+", "C-", "C+")
 
-    @pl.loop(0, 8)
+    @pl.loop(0, 1024 // BAND)
     def _(m):
-        band = pl.ds(pl.multiple_of(m * 128, 128), 128)
+        band = pl.ds(pl.multiple_of(m * BAND, BAND), BAND)
         right[band, :] = product(early, band, lambda k: panel[k])
         for lanes, value in gram_band(early, band):
             gram[band, lanes] = value
@@ -495,11 +501,11 @@
         ring.wait("A--")
         ring.wait("B++")
 
-    @pl.loop(0, 8)
+    @pl.loop(0, 1024 // BAND)
     def _(m):
-        band = pl.ds(pl.multiple_of(m * 128, 128), 128)
-        at = s * 1024 + m * 128 - start
-        eye = at + lax.broadcasted_iota(jnp.int32, (128, 512), 0) == lax.broadcasted_iota(jnp.int32, (128, 512), 1)
+        band = pl.ds(pl.multiple_of(m * BAND, BAND), BAND)
+        at = s * 1024 + m * BAND - start
+        eye = at + lax.broadcasted_iota(jnp.int32, (BAND, 512), 0) == lax.broadcasted_iota(jnp.int32, (BAND, 512), 1)
         block = right[band, :] + product(late, band, lambda k: panel[k]) + jnp.where(eye, shift, 0.0)
         white[band, :] = dot_split(block, inverse[...], ((1,), (1,))).astype(BF16)
 
@@ -514,9 +520,9 @@
     fs = exchange(16, lambda d: part_rows((s + d) % 16), lambda d: landed.at[d], f_send, f_recv, along)
     c_ring.siblings("A--", "B++", "C--")
 
-    @pl.loop(0, 8)
+    @pl.loop(0, 1024 // BAND)
     def _(m):
-        band = pl.ds(pl.multiple_of(m * 128, 128), 128)
+        band = pl.ds(pl.multiple_of(m * BAND, BAND), BAND)
         for lanes, value in gram_band(late, band):
             gram[band, lanes] = gram[band, lanes] + value
 
@@ -596,7 +602,7 @@
             dma((8,)), dma((8,)), dma((8,)), dma((8,)), dma((16,)), dma((16,)),
             dma((22,)), dma((22,)), dma((22,)), dma((22,)), dma((2, 22)), dma((2, 22)), dma((4,)), dma((4,)), dma((2,)), dma((5,)), dma((5,)),
             pltpu.VMEM((2048, 128), BF16), pltpu.VMEM((1, 2048), F32), pltpu.VMEM((8, 128), F32),
-            pltpu.VMEM((1024, 512), F32), dma((16,)), dma((16,)),
+            pltpu.VMEM((1024, 512), F32), pltpu.VMEM((128, 1024), F32), dma((16,)), dma((16,)),
         ],
         compiler_params=pltpu.CompilerParams(
             collective_id=0, has_side_effects=True, vmem_limit_bytes=36 * 1024 * 1024

time: 119 us -> 114 us (0.958)
  Pallas kernels: 109 us -> 104 us
    pallas_call x1, Pallas kernels: 109 us -> 104 us  [on_device(): pl.pallas_call(kernel, out_shape=(jax.ShapeDtypeStruct((1024, 2048), F32)...]
where the time goes in v3:
time: 114 us; the launch traced here: 113 us
  Pallas kernels  104 us (91%)
  local copies, waits for them, and re-layouts  7.76 us (7%)
  between operations  1.3 us (1%)
    pallas_call x1, Pallas kernels, on_device(): pl.pallas_call(kernel, out_shape=(jax.ShapeDtypeStruct((1024, 2048), F32)...  104 us
    unnamed x9, local copies, waits for them, and re-layouts  7.76 us

profile of v3, /device:TPU:1, one launch (start us, length us, event | category | flops | bytes accessed | tf_op | source)
XLA Modules:
  0.0 113.5 jit_solution(4858333598471172508)
XLA Ops:
  1.3 0.0 copy-start
  1.3 1.0 copy-done
  2.3 0.0 copy-start.1
  2.3 1.0 copy-done.1
  3.4 0.0 copy-start.2
  3.4 0.7 copy-done.2
  4.1 104.4 %whiten.1 = (f32[1024,2048]{1,0:T(8,128)S(1)}, bf16[1024,512]{1,0:T(8,128)(2,1)S(1)}, f32[32,256]{1,0:T(8,128)S(1)}) custom-call(bf16[128,2048]{1,0:T(8,128)(2,1)S(1)} %copy-done, f32[1,2048]{1,0:T(1,128)S(1)} %bitcast.3, s32[1]{0:T(128)S(6)} %copy.10.index, bf16[256,1024]{1,0:T(8,128)(2,1)S(1)} %copy-done.1), custom_call_target="tpu_custom_call" | custom-call | flops 12000000000 | bytes 20000000 | tf_op jit(solution)/shard_map/whiten/pallas_call | solution.py:569
  108.5 3.4 %copy.11 = f32[1024,2048]{1,0:T(8,128)} copy(f32[1024,2048]{1,0:T(8,128)S(1)} %get-tuple-element.12) | data formatting | bytes 16777216
  111.9 1.0 copy.12
  112.9 0.6 copy.13
Async XLA Ops:
  1.3 1.0 copy-start
  2.3 1.0 copy-start.1
  3.4 0.7 copy-start.2

commit v4 on v3

--- a/solution.py
+++ b/solution.py
@@ -387,8 +387,8 @@
         total = total + trace_t[d]
     trace_sum[...] = total
     ts = exchange(16, lambda d: trace_sum, lambda d: trace_s.at[d], ts_send, ts_recv, along)
+    relay_on(1)
     p_ring.step1()
-    relay_on(1)
     p_ring.step2()
     p_ring.step3()
     c_ring.step0()
@@ -512,7 +512,7 @@
     fetch[2].wait()
     for k in range(4):
         lanes = slice(k * 128, (k + 1) * 128)
-        part[lanes, :] = dot(white[:, lanes], weight[...], ((0,), (1,)))
+        part[lanes, :] = dot(white[:, lanes], weight[...], ((0,), (1,))).astype(BF16)
 
     def part_rows(k):
         return part.at[pl.ds(pl.multiple_of(k * 32, 32), 32)]
@@ -537,9 +537,9 @@
 
     for copy in fs:
         copy.wait_recv()
-    total = part[pl.ds(pl.multiple_of(s * 32, 32), 32), :]
+    total = part[pl.ds(pl.multiple_of(s * 32, 32), 32), :].astype(F32)
     for d in range(1, 16):
-        total = total + landed[d]
+        total = total + landed[d].astype(F32)
     proj_out[...] = total
 
     for copies in (sq, rs, gt, tt, ag, ts, fs):
@@ -584,8 +584,8 @@
             pltpu.VMEM((8, 256, 512), BF16),
             pltpu.VMEM((512, 1024), F32),
             pltpu.VMEM((512, 512), F32),
-            pltpu.VMEM((512, 256), F32),
-            pltpu.VMEM((16, 32, 256), F32),
+            pltpu.VMEM((512, 256), BF16),
+            pltpu.VMEM((16, 32, 256), BF16),
             pltpu.VMEM((2048, 128), BF16),
             pltpu.VMEM((8, 8, 128), F32),
             pltpu.VMEM((128, 512), BF16),

time: 114 us -> 112 us (0.982)
    pallas_call x1, Pallas kernels: 104 us -> 103 us  [on_device(): pl.pallas_call(kernel, out_shape=(jax.ShapeDtypeStruct((1024, 2048), F32)...]
where the time goes in v4:
time: 112 us
  Pallas kernels  103 us (92%)
  local copies, waits for them, and re-layouts  7.76 us (7%)
  between operations  1.3 us (1%)
    pallas_call x1, Pallas kernels, on_device(): pl.pallas_call(kernel, out_shape=(jax.ShapeDtypeStruct((1024, 2048), F32)...  103 us
    unnamed x9, local copies, waits for them, and re-layouts  7.76 us

profile of v4, /device:TPU:1, one launch (start us, length us, event | category | flops | bytes accessed | tf_op | source)
XLA Modules:
  0.0 111.6 jit_solution(8570786172204581835)
XLA Ops:
  1.3 0.0 copy-start
  1.3 1.0 copy-done
  2.3 0.0 copy-start.1
  2.3 1.0 copy-done.1
  3.4 0.0 copy-start.2
  3.4 0.7 copy-done.2
  4.1 102.6 %whiten.1 = (f32[1024,2048]{1,0:T(8,128)S(1)}, bf16[1024,512]{1,0:T(8,128)(2,1)S(1)}, f32[32,256]{1,0:T(8,128)S(1)}) custom-call(bf16[128,2048]{1,0:T(8,128)(2,1)S(1)} %copy-done, f32[1,2048]{1,0:T(1,128)S(1)} %bitcast.3, s32[1]{0:T(128)S(6)} %copy.10.index, bf16[256,1024]{1,0:T(8,128)(2,1)S(1)} %copy-done.1), custom_call_target="tpu_custom_call" | custom-call | flops 12000000000 | bytes 20000000 | tf_op jit(solution)/shard_map/whiten/pallas_call | solution.py:569
  106.6 3.4 %copy.11 = f32[1024,2048]{1,0:T(8,128)} copy(f32[1024,2048]{1,0:T(8,128)S(1)} %get-tuple-element.12) | data formatting | bytes 16777216
  110.0 1.0 copy.12
  111.0 0.6 copy.13
Async XLA Ops:
  1.3 1.0 copy-start
  2.3 1.0 copy-start.1
  3.4 0.7 copy-start.2

commit v5 on v4

--- a/solution.py
+++ b/solution.py
@@ -395,6 +395,8 @@
     landed_rows(0)
     r_ring[0].step0()
     p_ring.step4()
+    landed_rows(1)
+    r_ring[1].step0()
     p_ring.siblings("A", "B", "A-", "A+", "B-", "B+", "A--", "B++")
 
     for copy in ts:
@@ -418,8 +420,6 @@
         return 0
 
     lax.fori_loop(0, 4, fill, 0)
-    landed_rows(1)
-    r_ring[1].step0()
     c_ring.step1()
 
     far = (y + 2) % 4
@@ -474,10 +474,10 @@
             r_ring[1].step1()
             c_ring.step3()
             r_ring[1].step2()
+            r_ring[0].step3()
 
         @pl.when(b == 2)
         def _():
-            r_ring[0].step3()
             r_ring[1].step3()
             c_ring.step4()
 

time: 112 us -> 112 us (level)
  no operation moved by 1% of the time
where the time goes in v5:
time: 112 us
  Pallas kernels  103 us (92%)
  local copies, waits for them, and re-layouts  7.76 us (7%)
  between operations  1.3 us (1%)
    pallas_call x1, Pallas kernels, on_device(): pl.pallas_call(kernel, out_shape=(jax.ShapeDtypeStruct((1024, 2048), F32)...  103 us
    unnamed x9, local copies, waits for them, and re-layouts  7.76 us

profile of v5, /device:TPU:1, one launch (start us, length us, event | category | flops | bytes accessed | tf_op | source)
XLA Modules:
  0.0 111.6 jit_solution(14018693939492996282)
XLA Ops:
  1.3 0.0 copy-start
  1.3 1.0 copy-done
  2.3 0.0 copy-start.1
  2.3 1.0 copy-done.1
  3.4 0.0 copy-start.2
  3.4 0.7 copy-done.2
  4.1 102.6 %whiten.1 = (f32[1024,2048]{1,0:T(8,128)S(1)}, bf16[1024,512]{1,0:T(8,128)(2,1)S(1)}, f32[32,256]{1,0:T(8,128)S(1)}) custom-call(bf16[128,2048]{1,0:T(8,128)(2,1)S(1)} %copy-done, f32[1,2048]{1,0:T(1,128)S(1)} %bitcast.3, s32[1]{0:T(128)S(6)} %copy.10.index, bf16[256,1024]{1,0:T(8,128)(2,1)S(1)} %copy-done.1), custom_call_target="tpu_custom_call" | custom-call | flops 12000000000 | bytes 20000000 | tf_op jit(solution)/shard_map/whiten/pallas_call | solution.py:569
  106.7 3.4 %copy.11 = f32[1024,2048]{1,0:T(8,128)} copy(f32[1024,2048]{1,0:T(8,128)S(1)} %get-tuple-element.12) | data formatting | bytes 16777216
  110.1 1.0 copy.12
  111.0 0.6 copy.13
Async XLA Ops:
  1.3 1.0 copy-start
  2.3 1.0 copy-start.1
  3.4 0.7 copy-start.2
